TPU v7x, 32 devices: a whole 2x2x4 slice. The times are simulated.
32 devices in a mesh: gx: 16 (over z, y, core), gy: 2 (over x).
Axes of the slice: x: 2, y: 2, z: 4, core: 2. Of those that a mesh axis runs over, the one named last changes fastest.
Arguments:
- conserved: float32 [5, 16, 128, 256], P(None, None, 'gx', 'gy'), may hold values from -2.5 to 9, as said below
- register: float32 [5, 16, 128, 256], P(None, None, 'gx', 'gy'), may hold values from -1 to 1, as said below
- ghost_planes: float32 [5, 16, 128, 256], P(None, None, 'gx', 'gy'), may hold values from -2.5 to 9, as said below
Outputs:
- advanced: float32 [5, 16, 128, 256], P(None, None, 'gx', 'gy')
- carried: float32 [5, 16, 128, 256], P(None, None, 'gx', 'gy')
Inputs may be any that keep to these rules, and one draw needn't show every extreme that they name: `conserved`: every cell holds density in [0.6, 1.4], velocity components of magnitude at most 1.5 and T = 1.4 p / rho in [0.7, 1.4]; energy is E = p / 0.4 + 0.5 rho |u|^2. `ghost_planes`: every cell holds density in [0.6, 1.4], velocity components of magnitude at most 1.5 and T = 1.4 p / rho in [0.7, 1.4]; energy is E = p / 0.4 + 0.5 rho |u|^2. `register`: the density row lies in [-0.25, 0.25]; the momentum and energy rows lie in [-1, 1]. Density stays at 0.3 or more through both sections.
All inputs are finite; a program needn't handle non-finite values.
Results may differ from a plain program's by a relative error of at most 0.00002.
Values sent between devices are 32-bit elements; how exact they have to be, the bound alone decides.
A program may use at most 64 MiB of HBM per device.

v0:
```python
import jax
import jax.numpy as jnp
from jax import lax
from jax.sharding import PartitionSpec as P

adiabatic_exponent = 1.4
viscosity = 0.15
conductivity = 0.15 / (0.4 * 0.7)
time_step = 0.2
section_a = (-0.41789047, -1.19215169)
section_b = (0.37921031, 0.82295503)
stencil = (0.8, -0.2, 4.0 / 105.0, -1.0 / 280.0)


def padded_2(block, sides, width):
    for axis, dim in sides:
        count = lax.axis_size(axis)
        forward = [(i, i + 1) for i in range(count - 1)]
        forward.append((count - 1, 0))
        backward = [(target, source) for source, target in forward]
        low = lax.ppermute(
            lax.slice_in_dim(block, block.shape[dim] - width, None, axis=dim), axis, forward
        )
        high = lax.ppermute(lax.slice_in_dim(block, 0, width, axis=dim), axis, backward)
        block = jnp.concatenate([low, block, high], axis=dim)
    return block


def derivative(field, along):
    extent = field.shape[along]
    result = None
    for offset, weight in enumerate(stencil, start=1):
        term = weight * (
            lax.slice_in_dim(field, 4 + offset, extent - 4 + offset, axis=along)
            - lax.slice_in_dim(field, 4 - offset, extent - 4 - offset, axis=along)
        )
        result = term if result is None else result + term
    return result


def primitives(fields):
    density = fields[0]
    density = jnp.where(density == 0.0, 1.0, density)
    speeds = [fields[1] / density, fields[2] / density, fields[3] / density]
    kinetic = (
        0.5 * density * (speeds[0] * speeds[0] + speeds[1] * speeds[1] + speeds[2] * speeds[2])
    )
    pressure = (adiabatic_exponent - 1.0) * (fields[4] - kinetic)
    heat = adiabatic_exponent * pressure / density
    return speeds + [heat, pressure]


def window(items, planes, rows, columns):
    return [item[planes, rows, columns] for item in items]


def euler_flux(fields, primitive, direction):
    speed = primitive[direction]
    pressure = primitive[4]
    entries = [fields[1 + direction]]
    for index in range(3):
        entry = fields[1 + index] * speed
        if index == direction:
            entry = entry + pressure
        entries.append(entry)
    entries.append((fields[4] + pressure) * speed)
    return entries


def viscous_flux(grads, primitive, direction):
    dilation = grads[0] + grads[4] + grads[8]
    stresses = []
    for index in range(3):
        stress = viscosity * (grads[3 * index + direction] + grads[3 * direction + index])
        if index == direction:
            stress = stress - 2.0 / 3.0 * viscosity * dilation
        stresses.append(stress)
    energy = (
        primitive[0] * stresses[0]
        + primitive[1] * stresses[1]
        + primitive[2] * stresses[2]
        + conductivity * grads[9 + direction]
    )
    return stresses + [energy]


def net_flux(fields, primitive, viscous, direction):
    inviscid = euler_flux(fields, primitive, direction)
    return [inviscid[0]] + [inviscid[k + 1] - viscous[k] for k in range(4)]


def gradient_list(primitive, inner_x, inner_y):
    grads = []
    for quantity in range(4):
        field = primitive[quantity]
        grads.append(derivative(field[4:-4, :, inner_y], 1))
        grads.append(derivative(field[4:-4, inner_x, :], 2))
        grads.append(derivative(field[:, inner_x, inner_y], 0))
    return grads


def section_tendency(extended):
    whole = slice(None)
    inner = slice(4, -4)
    deep = slice(8, -8)
    padded = padded_2(extended, (("gx", 2), ("gy", 3)), 4)
    fields = [padded[k] for k in range(5)]
    primitive = primitives(fields)
    grads = gradient_list(primitive, inner, inner)
    visc_z = viscous_flux(grads, window(primitive, inner, inner, inner), 2)
    middle = [grad[4:-4] for grad in grads]
    grad_padded = padded_2(jnp.stack(middle, axis=0), (("gx", 2), ("gy", 3)), 4)
    visc_x = viscous_flux(
        [grad_padded[k, :, :, 4:-4] for k in range(12)], window(primitive, deep, whole, inner), 0
    )
    visc_y = viscous_flux(
        [grad_padded[k, :, 4:-4, :] for k in range(12)], window(primitive, deep, inner, whole), 1
    )
    cons_x = window(fields, deep, whole, inner)
    prim_x = window(primitive, deep, whole, inner)
    cons_y = window(fields, deep, inner, whole)
    prim_y = window(primitive, deep, inner, whole)
    cons_z = [extended[k, 4:-4] for k in range(5)]
    prim_z = window(primitive, inner, inner, inner)
    flux_x = net_flux(cons_x, prim_x, visc_x, 0)
    flux_y = net_flux(cons_y, prim_y, visc_y, 1)
    flux_z = net_flux(cons_z, prim_z, visc_z, 2)
    return jnp.stack(
        [
            -(derivative(flux_x[k], 1) + derivative(flux_y[k], 2) + derivative(flux_z[k], 0))
            for k in range(5)
        ],
        axis=0,
    )


def body(conserved, register, ghost_planes):
    ghost_half = ghost_planes.shape[1] // 2
    current = conserved
    for step_index in range(2):
        extended = jnp.concatenate(
            [ghost_planes[:, :ghost_half], current, ghost_planes[:, ghost_half:]], axis=1
        )
        tendency = section_tendency(extended)
        register = section_a[step_index] * register + time_step * tendency
        current = current + section_b[step_index] * register
    return (current, register)


def solution(mesh):
    return jax.shard_map(
        body,
        mesh=mesh,
        in_specs=(P(None, None, "gx", "gy"), P(None, None, "gx", "gy"), P(None, None, "gx", "gy")),
        out_specs=(P(None, None, "gx", "gy"), P(None, None, "gx", "gy")),
        check_vma=False,
    )
```

profile of v0, /device:TPU:0, one launch (start us, length us, event | category | flops | bytes accessed | tf_op | source)
XLA Modules:
  0.0 182.4 jit_solution(14034585683148129172)
XLA Ops:
  2.8 5.5 %collective-permute-start.1 = (f32[5,32,4,128]{3,1,2,0:T(8,128)S(1)}, f32[5,32,4,128]{3,1,2,0:T(8,128)S(1)}, u32[]{:S(2)}, u32[]{:S(2)}) collective-permute-start(f32[5,32,4,128]{3,1,2,0:T(8,128)S(1)} %copy.260), channel_id=1, source_target_pairs={{2,0},{4,2},{6,4},{8,6},{10,8},{12,10},{14,12},{16,14},{18,16},{20... | collective-permute-start | bytes 983048 | tf_op jit(solution)/shard_map/ppermute | solution.py:24
  8.4 4.5 %collective-permute-done.1 = f32[5,32,4,128]{3,1,2,0:T(8,128)S(1)} collective-permute-done((f32[5,32,4,128]{3,1,2,0:T(8,128)S(1)}, f32[5,32,4,128]{3,1,2,0:T(8,128)S(1)}, u32[]{:S(2)}, u32[]{:S(2)}) %collective-permute-start.1) | collective-permute-done | bytes 327712 | tf_op jit(solution)/shard_map/ppermute | solution.py:24
  13.2 4.5 %collective-permute-done = f32[5,32,4,128]{3,1,2,0:T(8,128)S(1)} collective-permute-done((f32[5,32,4,128]{3,1,2,0:T(8,128)S(1)}, f32[5,32,4,128]{3,1,2,0:T(8,128)S(1)}, u32[]{:S(2)}, u32[]{:S(2)}) %collective-permute-start) | collective-permute-done | bytes 327712 | tf_op jit(solution)/shard_map/ppermute | solution.py:21
  24.3 2.6 %collective-permute-done.3 = f32[5,32,16,4]{1,2,3,0:T(8,128)S(1)} collective-permute-done((f32[5,32,16,4]{1,2,3,0:T(8,128)S(1)}, f32[5,32,16,4]{1,2,3,0:T(8,128)S(1)}, u32[]{:S(2)}, u32[]{:S(2)}) %collective-permute-start.3) | collective-permute-done | bytes 40992 | tf_op jit(solution)/shard_map/ppermute | solution.py:24
  30.7 3.1 %fusion.3 = f32[5,32,16,136]{3,2,1,0:T(8,128)S(1)} fusion(f32[5,8,8,128]{3,2,1,0:T(8,128)S(1)} %get-tuple-element.133, f32[5,8,8,128]{3,2,1,0:T(8,128)S(1)} %get-tuple-element.132, f32[5,32,16,4]{3,2,1,0:T(8,128)S(1)} %copy.234, f32[5,32,4,128]{3,2,1,0:T(4,128)S(1)} %copy.230, f32[5,16,8,128]{3,2,1,0:T(8,128)S(1)} %copy-done.12, ...), kind=kLoop, calls=%fused_computation.7 | loop fusion | flops 2088960 | bytes 2785280 | tf_op jit(solution)/shard_map/concatenate | solution.py:25
  39.7 3.5 %fusion.164 = (f32[24,8,128]{2,1,0:T(8,128)}, f32[24,8,128]{2,1,0:T(8,128)}, f32[24,8,128]{2,1,0:T(8,128)S(1)}, f32[24,8,128]{2,1,0:T(8,128)S(1)}, f32[24,8,128]...) fusion(f32[32,16,136]{2,1,0:T(8,128)S(1)} %get-tuple-element.31, ...), kind=kLoop, calls=%fused_computation.343 | loop fusion | flops 2654208 | bytes 7667712 | tf_op jit(solution)/shard_map/sub | solution.py:89
  50.6 2.0 %fusion.169 = (f32[24,8,128]{2,1,0:T(8,128)}, f32[24,8,128]{2,1,0:T(8,128)}, f32[24,8,128]{2,1,0:T(8,128)}) fusion(f32[5,32,8,128]{3,2,1,0:T(8,128)} %copy-done.16, f32[32,16,136]{2,1,0:T(8,128)} %get-tuple-element.29, f32[32,16,136]{2,1,0:T(8,128)S(1)} %get-tuple-element.33, f32[24,8,128]{2,1,0:T(8,128)S(1)} %copy-done.55, ...), kind=kLoop, calls=%fused_computation.351 | loop fusion | flops 417792 | bytes 1474560 | tf_op jit(solution)/shard_map/sub | solution.py:89
  52.5 2.0 %collective-permute-done.5 = f32[12,16,4,128]{3,1,2,0:T(8,128)S(1)} collective-permute-done((f32[12,16,4,128]{3,1,2,0:T(8,128)S(1)}, f32[12,16,4,128]{3,1,2,0:T(8,128)S(1)}, u32[]{:S(2)}, u32[]{:S(2)}) %collective-permute-start.5) | collective-permute-done | bytes 393248 | tf_op jit(solution)/shard_map/ppermute | solution.py:24
  54.7 4.7 %collective-permute-done.4 = f32[12,16,4,128]{3,1,2,0:T(8,128)S(1)} collective-permute-done((f32[12,16,4,128]{3,1,2,0:T(8,128)S(1)}, f32[12,16,4,128]{3,1,2,0:T(8,128)S(1)}, u32[]{:S(2)}, u32[]{:S(2)}) %collective-permute-start.4) | collective-permute-done | bytes 393248 | tf_op jit(solution)/shard_map/ppermute | solution.py:21
  59.9 2.2 %fusion.589 = (f32[12,16,16,4]{3,2,1,0:T(8,128)}, f32[12,16,16,4]{3,2,1,0:T(8,128)}) fusion(f32[12,16,16,128]{3,2,1,0:T(8,128)S(1)} %pad_maximum_fusion.8), kind=kLoop, calls=%fused_computation.987 | loop fusion | bytes 196608 | tf_op jit(solution)/shard_map/slice | solution.py:22
  62.1 3.5 %copy.240 = f32[12,16,16,4]{2,1,3,0:T(8,128)} copy(f32[12,16,16,4]{3,2,1,0:T(8,128)} %get-tuple-element.49) | data formatting | bytes 98304 | tf_op jit(solution)/shard_map/slice | solution.py:24
  66.9 3.5 %copy.239 = f32[12,16,16,4]{2,1,3,0:T(8,128)} copy(f32[12,16,16,4]{3,2,1,0:T(8,128)} %get-tuple-element.48) | data formatting | bytes 98304 | tf_op jit(solution)/shard_map/slice | solution.py:22
  77.8 2.2 %copy.242 = f32[12,16,16,4]{3,2,1,0:T(8,128)S(1)} copy(f32[12,16,16,4]{2,1,3,0:T(8,128)} %collective-permute-done.7) | data formatting | bytes 98304 | tf_op jit(solution)/shard_map/ppermute | solution.py:24
  80.0 2.5 %collective-permute-done.6 = f32[12,16,16,4]{2,1,3,0:T(8,128)} collective-permute-done((f32[12,16,16,4]{2,1,3,0:T(8,128)}, f32[12,16,16,4]{2,1,3,0:T(8,128)}, u32[]{:S(2)}, u32[]{:S(2)}) %collective-permute-start.6) | collective-permute-done | bytes 49184 | tf_op jit(solution)/shard_map/ppermute | solution.py:21
  82.4 3.3 %copy.241 = f32[12,16,16,4]{3,2,1,0:T(8,128)} copy(f32[12,16,16,4]{2,1,3,0:T(8,128)} %collective-permute-done.6) | data formatting | bytes 98304 | tf_op jit(solution)/shard_map/ppermute | solution.py:21
  90.3 1.9 %fusion.58 = f32[16,8,136]{2,1,0:T(8,128)S(1)} fusion(f32[12,16,16,4]{3,2,1,0:T(8,128)S(1)} %copy.242, f32[12,16,16,4]{3,2,1,0:T(8,128)S(1)} %copy-done, f32[12,16,4,128]{3,2,1,0:T(4,128)S(1)} %copy.238, f32[12,16,8,128]{3,2,1,0:T(8,128)S(1)} %constant_dynamic-update-slice_fusion, f32[12,16,4,128]{3,2,1,0:T(4,128)S(1)} %copy.237, ...), kind=kLoop, calls=%fused_computation.156 | loop fusion | flops 905216 | bytes 2088960 | tf_op jit(solution)/shard_map/sub | solution.py:89
  96.1 3.8 %collective-permute-done.9 = f32[5,32,4,128]{3,1,2,0:T(8,128)S(1)} collective-permute-done((f32[5,32,4,128]{3,1,2,0:T(8,128)S(1)}, f32[5,32,4,128]{3,1,2,0:T(8,128)S(1)}, u32[]{:S(2)}, u32[]{:S(2)}) %collective-permute-start.9) | collective-permute-done | bytes 327712 | tf_op jit(solution)/shard_map/ppermute | solution.py:24
  100.1 4.7 %collective-permute-done.8 = f32[5,32,4,128]{3,1,2,0:T(8,128)S(1)} collective-permute-done((f32[5,32,4,128]{3,1,2,0:T(8,128)S(1)}, f32[5,32,4,128]{3,1,2,0:T(8,128)S(1)}, u32[]{:S(2)}, u32[]{:S(2)}) %collective-permute-start.8) | collective-permute-done | bytes 327712 | tf_op jit(solution)/shard_map/ppermute | solution.py:21
  105.3 1.9 %fusion.590 = (f32[5,32,16,4]{3,2,1,0:T(8,128)}, f32[5,32,16,4]{3,2,1,0:T(8,128)}) fusion(f32[5,32,16,128]{3,2,1,0:T(8,128)S(1)} %fusion.11), kind=kLoop, calls=%fused_computation.988 | loop fusion | bytes 163840 | tf_op jit(solution)/shard_map/slice | solution.py:22
  107.2 2.0 %copy.248 = f32[5,32,16,4]{1,2,3,0:T(8,128)S(1)} copy(f32[5,32,16,4]{3,2,1,0:T(8,128)} %get-tuple-element.51) | data formatting | bytes 81920 | tf_op jit(solution)/shard_map/slice | solution.py:24
  112.0 2.6 %collective-permute-done.11 = f32[5,32,16,4]{1,2,3,0:T(8,128)S(1)} collective-permute-done((f32[5,32,16,4]{1,2,3,0:T(8,128)S(1)}, f32[5,32,16,4]{1,2,3,0:T(8,128)S(1)}, u32[]{:S(2)}, u32[]{:S(2)}) %collective-permute-start.11) | collective-permute-done | bytes 40992 | tf_op jit(solution)/shard_map/ppermute | solution.py:24
  118.4 3.1 %fusion.7 = f32[5,32,16,136]{3,2,1,0:T(8,128)S(1)} fusion(f32[5,8,8,128]{3,2,1,0:T(8,128)S(1)} %get-tuple-element.133, f32[5,8,8,128]{3,2,1,0:T(8,128)S(1)} %get-tuple-element.132, f32[5,32,16,4]{3,2,1,0:T(8,128)S(1)} %copy.250, f32[5,32,4,128]{3,2,1,0:T(4,128)S(1)} %copy.246, f32[5,16,8,128]{3,2,1,0:T(8,128)S(1)} %multiply_add_fusion.2, ...), kind=kLoop, calls=%fused_computation.11 | loop fusion | flops 2088960 | bytes 2785280 | tf_op jit(solution)/shard_map/concatenate | solution.py:25
  128.3 3.5 %fusion.95 = (f32[24,8,128]{2,1,0:T(8,128)}, f32[24,8,128]{2,1,0:T(8,128)}, f32[24,8,128]{2,1,0:T(8,128)S(1)}, f32[24,8,128]{2,1,0:T(8,128)S(1)}, f32[24,8,128]{...) fusion(f32[32,16,136]{2,1,0:T(8,128)S(1)} %get-tuple-element.17, ...), kind=kLoop, calls=%fused_computation.236 | loop fusion | flops 2654208 | bytes 7667712 | tf_op jit(solution)/shard_map/sub | solution.py:89
  140.1 2.2 %collective-permute-done.13 = f32[12,16,4,128]{3,1,2,0:T(8,128)S(1)} collective-permute-done((f32[12,16,4,128]{3,1,2,0:T(8,128)S(1)}, f32[12,16,4,128]{3,1,2,0:T(8,128)S(1)}, u32[]{:S(2)}, u32[]{:S(2)}) %collective-permute-start.13) | collective-permute-done | bytes 393248 | tf_op jit(solution)/shard_map/ppermute | solution.py:24
  142.4 4.8 %collective-permute-done.12 = f32[12,16,4,128]{3,1,2,0:T(8,128)S(1)} collective-permute-done((f32[12,16,4,128]{3,1,2,0:T(8,128)S(1)}, f32[12,16,4,128]{3,1,2,0:T(8,128)S(1)}, u32[]{:S(2)}, u32[]{:S(2)}) %collective-permute-start.12) | collective-permute-done | bytes 393248 | tf_op jit(solution)/shard_map/ppermute | solution.py:21
  147.7 2.2 %fusion.588 = (f32[12,16,16,4]{3,2,1,0:T(8,128)}, f32[12,16,16,4]{3,2,1,0:T(8,128)}) fusion(f32[12,16,16,128]{3,2,1,0:T(8,128)S(1)} %pad_maximum_fusion.9), kind=kLoop, calls=%fused_computation.986 | loop fusion | bytes 196608 | tf_op jit(solution)/shard_map/slice | solution.py:22
  149.9 3.5 %copy.256 = f32[12,16,16,4]{2,1,3,0:T(8,128)} copy(f32[12,16,16,4]{3,2,1,0:T(8,128)} %get-tuple-element.47) | data formatting | bytes 98304 | tf_op jit(solution)/shard_map/slice | solution.py:24
  154.4 3.5 %copy.255 = f32[12,16,16,4]{2,1,3,0:T(8,128)} copy(f32[12,16,16,4]{3,2,1,0:T(8,128)} %get-tuple-element.46) | data formatting | bytes 98304 | tf_op jit(solution)/shard_map/slice | solution.py:22
  165.1 2.2 %copy.258 = f32[12,16,16,4]{3,2,1,0:T(8,128)S(1)} copy(f32[12,16,16,4]{2,1,3,0:T(8,128)} %collective-permute-done.15) | data formatting | bytes 98304 | tf_op jit(solution)/shard_map/ppermute | solution.py:24
  167.3 2.0 %collective-permute-done.14 = f32[12,16,16,4]{2,1,3,0:T(8,128)} collective-permute-done((f32[12,16,16,4]{2,1,3,0:T(8,128)}, f32[12,16,16,4]{2,1,3,0:T(8,128)}, u32[]{:S(2)}, u32[]{:S(2)}) %collective-permute-start.14) | collective-permute-done | bytes 49184 | tf_op jit(solution)/shard_map/ppermute | solution.py:21
  169.3 3.3 %copy.257 = f32[12,16,16,4]{3,2,1,0:T(8,128)} copy(f32[12,16,16,4]{2,1,3,0:T(8,128)} %collective-permute-done.14) | data formatting | bytes 98304 | tf_op jit(solution)/shard_map/ppermute | solution.py:21
  177.2 1.9 %fusion.21 = f32[16,8,136]{2,1,0:T(8,128)S(1)} fusion(f32[12,16,16,4]{3,2,1,0:T(8,128)S(1)} %copy.258, f32[12,16,16,4]{3,2,1,0:T(8,128)S(1)} %copy-done.1, f32[12,16,4,128]{3,2,1,0:T(4,128)S(1)} %copy.254, f32[12,16,8,128]{3,2,1,0:T(8,128)S(1)} %constant_dynamic-update-slice_fusion.17, f32[12,16,4,128]{3,2,1,0:T(4,128)S(1)} %copy.253, ...), kind=kLoop, calls=%fused_computation.76 | loop fusion | flops 905216 | bytes 2088960 | tf_op jit(solution)/shard_map/sub | solution.py:89
  (314 shorter events, 81.5 us)
Async XLA Ops:
  2.7 10.5 %copy-start.16 = (f32[5,32,8,128]{3,2,1,0:T(8,128)}, f32[5,32,8,128]{3,2,1,0:T(8,128)S(1)}, u32[]{:S(2)}) copy-start(f32[5,32,8,128]{3,2,1,0:T(8,128)S(1)} %pad_maximum_fusion.11) | copy-start | bytes 1966084
  2.8 15.0 %copy-start.12 = (f32[5,16,8,128]{3,2,1,0:T(8,128)S(1)}, f32[5,16,8,128]{3,2,1,0:T(8,128)}, u32[]{:S(2)}) copy-start(f32[5,16,8,128]{3,2,1,0:T(8,128)} %param.3) | copy-start | bytes 983044
  2.8 10.1 %collective-permute-start.1 = (f32[5,32,4,128]{3,1,2,0:T(8,128)S(1)}, f32[5,32,4,128]{3,1,2,0:T(8,128)S(1)}, u32[]{:S(2)}, u32[]{:S(2)}) collective-permute-start(f32[5,32,4,128]{3,1,2,0:T(8,128)S(1)} %copy.260), channel_id=1, source_target_pairs={{2,0},{4,2},{6,4},{8,6},{10,8},{12,10},{14,12},{16,14},{18,16},{20... | collective-permute-start | bytes 983048 | tf_op jit(solution)/shard_map/ppermute | solution.py:24
  8.4 9.2 %collective-permute-start = (f32[5,32,4,128]{3,1,2,0:T(8,128)S(1)}, f32[5,32,4,128]{3,1,2,0:T(8,128)S(1)}, u32[]{:S(2)}, u32[]{:S(2)}) collective-permute-start(f32[5,32,4,128]{3,1,2,0:T(8,128)S(1)} %copy.259), channel_id=1, source_target_pairs={{0,2},{2,4},{4,6},{6,8},{8,10},{10,12},{12,14},{14,16},{16,18},{18... | collective-permute-start | bytes 983048 | tf_op jit(solution)/shard_map/ppermute | solution.py:21
  21.5 5.4 %collective-permute-start.3 = (f32[5,32,16,4]{1,2,3,0:T(8,128)S(1)}, f32[5,32,16,4]{1,2,3,0:T(8,128)S(1)}, u32[]{:S(2)}, u32[]{:S(2)}) collective-permute-start(f32[5,32,16,4]{1,2,3,0:T(8,128)S(1)} %copy.232), channel_id=1, source_target_pairs={{1,0},{0,1},{3,2},{2,3},{5,4},{4,5},{7,6},{6,7},{9,8},{8,9},{11,10... | collective-permute-start | bytes 122888 | tf_op jit(solution)/shard_map/ppermute | solution.py:24
  23.7 5.4 %collective-permute-start.2 = (f32[5,32,16,4]{1,2,3,0:T(8,128)S(1)}, f32[5,32,16,4]{1,2,3,0:T(8,128)S(1)}, u32[]{:S(2)}, u32[]{:S(2)}) collective-permute-start(f32[5,32,16,4]{1,2,3,0:T(8,128)S(1)} %copy.231), channel_id=1, source_target_pairs={{0,1},{1,0},{2,3},{3,2},{4,5},{5,4},{6,7},{7,6},{8,9},{9,8},{10,11... | collective-permute-start | bytes 122888 | tf_op jit(solution)/shard_map/ppermute | solution.py:21
  36.5 36.4 %copy-start.4 = (f32[32,16,136]{2,1,0:T(8,128)}, f32[32,16,136]{2,1,0:T(8,128)S(1)}, u32[]{:S(2)}) copy-start(f32[32,16,136]{2,1,0:T(8,128)S(1)} %get-tuple-element.31) | copy-start | bytes 835588
  36.5 36.4 %copy-start.9 = (f32[32,16,136]{2,1,0:T(8,128)}, f32[32,16,136]{2,1,0:T(8,128)S(1)}, u32[]{:S(2)}) copy-start(f32[32,16,136]{2,1,0:T(8,128)S(1)} %get-tuple-element.33) | copy-start | bytes 835588
  36.5 38.3 %copy-start.7 = (f32[32,16,136]{2,1,0:T(8,128)}, f32[32,16,136]{2,1,0:T(8,128)S(1)}, u32[]{:S(2)}) copy-start(f32[32,16,136]{2,1,0:T(8,128)S(1)} %get-tuple-element.32) | copy-start | bytes 835588
  43.2 4.8 %copy-start.56 = (f32[24,8,128]{2,1,0:T(8,128)}, f32[24,8,128]{2,1,0:T(8,128)S(1)}, u32[]{:S(2)}) copy-start(f32[24,8,128]{2,1,0:T(8,128)S(1)} %get-tuple-element.23) | copy-start | bytes 294916
  43.2 4.8 %copy-start.58 = (f32[24,8,128]{2,1,0:T(8,128)}, f32[24,8,128]{2,1,0:T(8,128)S(1)}, u32[]{:S(2)}) copy-start(f32[24,8,128]{2,1,0:T(8,128)S(1)} %get-tuple-element.24) | copy-start | bytes 294916
  43.2 4.8 %copy-start.60 = (f32[24,8,128]{2,1,0:T(8,128)}, f32[24,8,128]{2,1,0:T(8,128)S(1)}, u32[]{:S(2)}) copy-start(f32[24,8,128]{2,1,0:T(8,128)S(1)} %get-tuple-element.25) | copy-start | bytes 294916
  48.3 6.2 %collective-permute-start.5 = (f32[12,16,4,128]{3,1,2,0:T(8,128)S(1)}, f32[12,16,4,128]{3,1,2,0:T(8,128)S(1)}, u32[]{:S(2)}, u32[]{:S(2)}) collective-permute-start(f32[12,16,4,128]{3,1,2,0:T(8,128)S(1)} %copy.236), channel_id=1, source_target_pairs={{2,0},{4,2},{6,4},{8,6},{10,8},{12,10},{14,12},{16,14},{18,16},{20... | collective-permute-start | bytes 1179656 | tf_op jit(solution)/shard_map/ppermute | solution.py:24
  49.3 10.1 %collective-permute-start.4 = (f32[12,16,4,128]{3,1,2,0:T(8,128)S(1)}, f32[12,16,4,128]{3,1,2,0:T(8,128)S(1)}, u32[]{:S(2)}, u32[]{:S(2)}) collective-permute-start(f32[12,16,4,128]{3,1,2,0:T(8,128)S(1)} %copy.235), channel_id=1, source_target_pairs={{0,2},{2,4},{4,6},{6,8},{8,10},{10,12},{12,14},{14,16},{16,18},{18... | collective-permute-start | bytes 1179656 | tf_op jit(solution)/shard_map/ppermute | solution.py:21
  65.5 12.2 %collective-permute-start.7 = (f32[12,16,16,4]{2,1,3,0:T(8,128)}, f32[12,16,16,4]{2,1,3,0:T(8,128)}, u32[]{:S(2)}, u32[]{:S(2)}) collective-permute-start(f32[12,16,16,4]{2,1,3,0:T(8,128)} %copy.240), channel_id=1, source_target_pairs={{1,0},{0,1},{3,2},{2,3},{5,4},{4,5},{7,6},{6,7},{9,8},{8,9},{11,10... | collective-permute-start | bytes 147464 | tf_op jit(solution)/shard_map/ppermute | solution.py:24
  70.3 12.1 %collective-permute-start.6 = (f32[12,16,16,4]{2,1,3,0:T(8,128)}, f32[12,16,16,4]{2,1,3,0:T(8,128)}, u32[]{:S(2)}, u32[]{:S(2)}) collective-permute-start(f32[12,16,16,4]{2,1,3,0:T(8,128)} %copy.239), channel_id=1, source_target_pairs={{0,1},{1,0},{2,3},{3,2},{4,5},{5,4},{6,7},{7,6},{8,9},{9,8},{10,11... | collective-permute-start | bytes 147464 | tf_op jit(solution)/shard_map/ppermute | solution.py:21
  94.6 43.3 %copy-start.10 = (f32[5,16,8,128]{3,2,1,0:T(8,128)}, f32[5,16,8,128]{3,2,1,0:T(8,128)S(1)}, u32[]{:S(2)}) copy-start(f32[5,16,8,128]{3,2,1,0:T(8,128)S(1)} %multiply_add_fusion.2) | copy-start | bytes 983044
  94.7 5.5 %copy-start.15 = (f32[5,32,8,128]{3,2,1,0:T(8,128)}, f32[5,32,8,128]{3,2,1,0:T(8,128)S(1)}, u32[]{:S(2)}) copy-start(f32[5,32,8,128]{3,2,1,0:T(8,128)S(1)} %pad_maximum_fusion.10) | copy-start | bytes 1966084
  95.3 4.7 %collective-permute-start.9 = (f32[5,32,4,128]{3,1,2,0:T(8,128)S(1)}, f32[5,32,4,128]{3,1,2,0:T(8,128)S(1)}, u32[]{:S(2)}, u32[]{:S(2)}) collective-permute-start(f32[5,32,4,128]{3,1,2,0:T(8,128)S(1)} %copy.262), channel_id=1, source_target_pairs={{2,0},{4,2},{6,4},{8,6},{10,8},{12,10},{14,12},{16,14},{18,16},{20... | collective-permute-start | bytes 983048 | tf_op jit(solution)/shard_map/ppermute | solution.py:24
  95.4 9.5 %collective-permute-start.8 = (f32[5,32,4,128]{3,1,2,0:T(8,128)S(1)}, f32[5,32,4,128]{3,1,2,0:T(8,128)S(1)}, u32[]{:S(2)}, u32[]{:S(2)}) collective-permute-start(f32[5,32,4,128]{3,1,2,0:T(8,128)S(1)} %copy.261), channel_id=1, source_target_pairs={{0,2},{2,4},{4,6},{6,8},{8,10},{10,12},{12,14},{14,16},{16,18},{18... | collective-permute-start | bytes 983048 | tf_op jit(solution)/shard_map/ppermute | solution.py:21
  109.2 5.4 %collective-permute-start.11 = (f32[5,32,16,4]{1,2,3,0:T(8,128)S(1)}, f32[5,32,16,4]{1,2,3,0:T(8,128)S(1)}, u32[]{:S(2)}, u32[]{:S(2)}) collective-permute-start(f32[5,32,16,4]{1,2,3,0:T(8,128)S(1)} %copy.248), channel_id=1, source_target_pairs={{1,0},{0,1},{3,2},{2,3},{5,4},{4,5},{7,6},{6,7},{9,8},{8,9},{11,10... | collective-permute-start | bytes 122888 | tf_op jit(solution)/shard_map/ppermute | solution.py:24
  111.4 5.4 %collective-permute-start.10 = (f32[5,32,16,4]{1,2,3,0:T(8,128)S(1)}, f32[5,32,16,4]{1,2,3,0:T(8,128)S(1)}, u32[]{:S(2)}, u32[]{:S(2)}) collective-permute-start(f32[5,32,16,4]{1,2,3,0:T(8,128)S(1)} %copy.247), channel_id=1, source_target_pairs={{0,1},{1,0},{2,3},{3,2},{4,5},{5,4},{6,7},{7,6},{8,9},{9,8},{10,11... | collective-permute-start | bytes 122888 | tf_op jit(solution)/shard_map/ppermute | solution.py:21
  124.2 36.6 %copy-start.2 = (f32[32,16,136]{2,1,0:T(8,128)}, f32[32,16,136]{2,1,0:T(8,128)S(1)}, u32[]{:S(2)}) copy-start(f32[32,16,136]{2,1,0:T(8,128)S(1)} %get-tuple-element.17) | copy-start | bytes 835588
  124.2 36.6 %copy-start.8 = (f32[32,16,136]{2,1,0:T(8,128)}, f32[32,16,136]{2,1,0:T(8,128)S(1)}, u32[]{:S(2)}) copy-start(f32[32,16,136]{2,1,0:T(8,128)S(1)} %get-tuple-element.19) | copy-start | bytes 835588
  124.2 38.5 %copy-start.6 = (f32[32,16,136]{2,1,0:T(8,128)}, f32[32,16,136]{2,1,0:T(8,128)S(1)}, u32[]{:S(2)}) copy-start(f32[32,16,136]{2,1,0:T(8,128)S(1)} %get-tuple-element.18) | copy-start | bytes 835588
  131.8 4.8 %copy-start.45 = (f32[24,8,128]{2,1,0:T(8,128)}, f32[24,8,128]{2,1,0:T(8,128)S(1)}, u32[]{:S(2)}) copy-start(f32[24,8,128]{2,1,0:T(8,128)S(1)} %get-tuple-element.9) | copy-start | bytes 294916
  131.8 4.8 %copy-start.47 = (f32[24,8,128]{2,1,0:T(8,128)}, f32[24,8,128]{2,1,0:T(8,128)S(1)}, u32[]{:S(2)}) copy-start(f32[24,8,128]{2,1,0:T(8,128)S(1)} %get-tuple-element.10) | copy-start | bytes 294916
  131.8 4.8 %copy-start.49 = (f32[24,8,128]{2,1,0:T(8,128)}, f32[24,8,128]{2,1,0:T(8,128)S(1)}, u32[]{:S(2)}) copy-start(f32[24,8,128]{2,1,0:T(8,128)S(1)} %get-tuple-element.11) | copy-start | bytes 294916
  136.9 5.4 %collective-permute-start.13 = (f32[12,16,4,128]{3,1,2,0:T(8,128)S(1)}, f32[12,16,4,128]{3,1,2,0:T(8,128)S(1)}, u32[]{:S(2)}, u32[]{:S(2)}) collective-permute-start(f32[12,16,4,128]{3,1,2,0:T(8,128)S(1)} %copy.252), channel_id=1, source_target_pairs={{2,0},{4,2},{6,4},{8,6},{10,8},{12,10},{14,12},{16,14},{18,16},{20... | collective-permute-start | bytes 1179656 | tf_op jit(solution)/shard_map/ppermute | solution.py:24
  137.0 10.2 %collective-permute-start.12 = (f32[12,16,4,128]{3,1,2,0:T(8,128)S(1)}, f32[12,16,4,128]{3,1,2,0:T(8,128)S(1)}, u32[]{:S(2)}, u32[]{:S(2)}) collective-permute-start(f32[12,16,4,128]{3,1,2,0:T(8,128)S(1)} %copy.251), channel_id=1, source_target_pairs={{0,2},{2,4},{4,6},{6,8},{8,10},{10,12},{12,14},{14,16},{16,18},{18... | collective-permute-start | bytes 1179656 | tf_op jit(solution)/shard_map/ppermute | solution.py:21
  153.4 11.8 %collective-permute-start.15 = (f32[12,16,16,4]{2,1,3,0:T(8,128)}, f32[12,16,16,4]{2,1,3,0:T(8,128)}, u32[]{:S(2)}, u32[]{:S(2)}) collective-permute-start(f32[12,16,16,4]{2,1,3,0:T(8,128)} %copy.256), channel_id=1, source_target_pairs={{1,0},{0,1},{3,2},{2,3},{5,4},{4,5},{7,6},{6,7},{9,8},{8,9},{11,10... | collective-permute-start | bytes 147464 | tf_op jit(solution)/shard_map/ppermute | solution.py:24
  157.9 11.4 %collective-permute-start.14 = (f32[12,16,16,4]{2,1,3,0:T(8,128)}, f32[12,16,16,4]{2,1,3,0:T(8,128)}, u32[]{:S(2)}, u32[]{:S(2)}) collective-permute-start(f32[12,16,16,4]{2,1,3,0:T(8,128)} %copy.255), channel_id=1, source_target_pairs={{0,1},{1,0},{2,3},{3,2},{4,5},{5,4},{6,7},{7,6},{8,9},{9,8},{10,11... | collective-permute-start | bytes 147464 | tf_op jit(solution)/shard_map/ppermute | solution.py:21
  (84 other events, 246.4 us)
where the time goes:
time: 184 us; the launch traced here: 182 us
  local copies, waits for them, and re-layouts  64.3 us (35%)
  other arithmetic  53.4 us (29%)
  waiting for transfers between devices  45.7 us (25%)
  starting transfers between devices  16.7 us (9%)
  between operations  2.25 us (1%)
    sub x18, other arithmetic, net_flux(): return [inviscid[0]] + [inviscid[k + 1] - viscous[k] for k in range(4)]  33.4 us
    ppermute x8, waiting for transfers between devices, padded_2(): lax.ppermute(lax.slice_in_dim(block, block.shape[dim] - width, None, axis...  26.2 us
    ppermute x8, waiting for transfers between devices, padded_2(): lax.ppermute(lax.slice_in_dim(block, 0, width, axis=dim), axis, backward)  19.5 us
    slice x14, local copies, waits for them, and re-layouts, padded_2(): lax.slice_in_dim(block, block.shape[dim] - width, None, axis=dim)  16.6 us
    ppermute x8, starting transfers between devices, padded_2(): lax.ppermute(lax.slice_in_dim(block, 0, width, axis=dim), axis, backward)  12 us
    slice x6, local copies, waits for them, and re-layouts, padded_2(): lax.slice_in_dim(block, 0, width, axis=dim)  10.9 us
    ppermute x8, local copies, waits for them, and re-layouts, padded_2(): lax.ppermute(lax.slice_in_dim(block, block.shape[dim] - width, None, axis...  10.7 us
    unnamed x218, local copies, waits for them, and re-layouts  8.65 us
  transfers between devices with their start and end apart: 16, of which 16 were waited for; matrix products, arithmetic and copies ran while one was open for 17% of the time, Pallas kernels for 0%

commit v1 on v0

v1 whole, which is shorter than its diff:
```python
import functools

import jax
import jax.numpy as jnp
from jax import lax
from jax.experimental import pallas as pl
from jax.experimental.pallas import tpu as pltpu
from jax.sharding import PartitionSpec as P

MESH = pl.DeviceIdType.MESH

viscosity = 0.15
conductivity = 0.15 / (0.4 * 0.7)
time_step = 0.2
section_a = (-0.41789047, -1.19215169)
section_b = (0.37921031, 0.82295503)
stencil = (0.8, -0.2, 4.0 / 105.0, -1.0 / 280.0)
CH = 4


def kernel(
    nx,
    ny,
    chunks,
    cons_hbm,
    reg_hbm,
    ghost_hbm,
    adv_hbm,
    car_hbm,
    QE,
    PR,
    REG,
    FX,
    FY,
    FZ,
    GH,
    XS,
    XR,
    YS,
    YR,
    XSG,
    XRG,
    YSG,
    YRG,
    in_sem,
    out_sem,
    xs_sem,
    xr_sem,
    ys_sem,
    yr_sem,
    gs_sem,
    gr_sem,
):
    ix = lax.axis_index("gx")
    iy = lax.axis_index("gy")
    right = lax.rem(ix + 1, nx)
    left = lax.rem(ix + nx - 1, nx)
    up = lax.rem(iy + 1, ny)
    down = lax.rem(iy + ny - 1, ny)
    y_sides = (0,) if ny == 2 else (0, 1)

    planes = chunks * CH
    ghost = ghost_hbm.shape[1] // 2
    loads = [
        pltpu.make_async_copy(cons_hbm, QE.at[:, pl.ds(ghost, planes)], in_sem.at[0]),
        pltpu.make_async_copy(ghost_hbm.at[:, pl.ds(0, ghost)], QE.at[:, pl.ds(0, ghost)], in_sem.at[1]),
        pltpu.make_async_copy(
            ghost_hbm.at[:, pl.ds(ghost, ghost)], QE.at[:, pl.ds(ghost + planes, ghost)], in_sem.at[2]
        ),
        pltpu.make_async_copy(reg_hbm, REG, in_sem.at[3]),
    ]
    for load in loads:
        load.start()

    barrier = pltpu.get_barrier_semaphore()
    pl.semaphore_signal(barrier, inc=1, device_id={"gx": left}, device_id_type=MESH)
    pl.semaphore_signal(barrier, inc=1, device_id={"gx": right}, device_id_type=MESH)
    for side in y_sides:
        pl.semaphore_signal(barrier, inc=1, device_id={"gy": (up, down)[side]}, device_id_type=MESH)

    sub = lax.broadcasted_iota(jnp.int32, (8, 128), 0)
    lane = lax.broadcasted_iota(jnp.int32, (8, 128), 1)
    low = sub < 4
    lane_group = lax.shift_right_logical(lane, 3)
    lane_first = lax.bitwise_and(lane, 7) < 4

    def x_send(way, r, c, fields):
        return pltpu.make_async_remote_copy(
            src_ref=XS.at[way, r, c, pl.ds(0, fields)],
            dst_ref=XR.at[way, r, c, pl.ds(0, fields)],
            send_sem=xs_sem.at[way, r, c],
            recv_sem=xr_sem.at[way, r, c],
            device_id={"gx": (right, left)[way]},
            device_id_type=MESH,
        )

    def y_send(way, r, c, count):
        return pltpu.make_async_remote_copy(
            src_ref=YS.at[r, c, pl.ds(0, count)],
            dst_ref=YR.at[way, r, c, pl.ds(0, count)],
            send_sem=ys_sem.at[way, r, c],
            recv_sem=yr_sem.at[way, r, c],
            device_id={"gy": (up, down)[way]},
            device_id_type=MESH,
        )

    def xg_send(way):
        return pltpu.make_async_remote_copy(
            src_ref=XSG.at[way],
            dst_ref=XRG.at[way],
            send_sem=gs_sem.at[way],
            recv_sem=gr_sem.at[way],
            device_id={"gx": (right, left)[way]},
            device_id_type=MESH,
        )

    def yg_send(way):
        return pltpu.make_async_remote_copy(
            src_ref=YSG,
            dst_ref=YRG.at[way],
            send_sem=gs_sem.at[2 + way],
            recv_sem=gr_sem.at[2 + way],
            device_id={"gy": (up, down)[way]},
            device_id_type=MESH,
        )

    def exchange(r, c):
        fields, count = ((4, 1), (5, 2))[r % 2]
        return [x_send(way, r, c, fields) for way in (0, 1)] + [y_send(way, r, c, count) for way in y_sides]

    def ghost_exchange():
        return [xg_send(way) for way in (0, 1)] + [yg_send(way) for way in y_sides]

    def pack_high(first, second):
        return jnp.where(low, pltpu.roll(second, 4, 0), first)

    def pack_low(first, second):
        return jnp.where(low, first, pltpu.roll(second, 4, 0))

    def unpack_x(from_left, from_right):
        first = jnp.where(low, from_right, from_left)
        second = pltpu.roll(jnp.where(low, from_left, from_right), 4, 0)
        return first, second

    def pack_y(items):
        packed = None
        for j, item in enumerate(items):
            turned = pltpu.roll(item, (8 * j + 4) % 128, 1)
            packed = turned if packed is None else jnp.where(lane_group == j, turned, packed)
        return packed

    def merge_y(ref, *index):
        if ny == 2:
            return ref[(0,) + index]
        return jnp.where(lane_first, ref[(0,) + index], ref[(1,) + index])

    def unpack_y(merged, j):
        return pltpu.roll(merged, (128 - (8 * j + 4)) % 128, 1)

    def d_x(field, halo):
        total = None
        for s, weight in enumerate(stencil[:3], start=1):
            plus = pltpu.roll(jnp.where(sub < s, halo, field), 8 - s, 0)
            minus = pltpu.roll(jnp.where(sub >= 8 - s, halo, field), s, 0)
            term = weight * (plus - minus)
            total = term if total is None else total + term
        gap = halo - field
        return total + stencil[3] * pltpu.roll(jnp.where(low, gap, -gap), 4, 0)

    def d_y(field, halo):
        total = None
        for s, weight in enumerate(stencil, start=1):
            plus = pltpu.roll(jnp.where(lane < s, halo, field), 128 - s, 1)
            minus = pltpu.roll(jnp.where(lane >= 128 - s, halo, field), s, 1)
            term = weight * (plus - minus)
            total = term if total is None else total + term
        return total

    def d_z(ref, f, z):
        total = None
        for s, weight in enumerate(stencil, start=1):
            term = weight * (ref[f, z + s] - ref[f, z - s])
            total = term if total is None else total + term
        return total

    def primitives(q):
        inverse = 1.0 / q[0]
        speeds = [q[1] * inverse, q[2] * inverse, q[3] * inverse]
        kinetic = 0.5 * (q[1] * speeds[0] + q[2] * speeds[1] + q[3] * speeds[2])
        pressure = 0.4 * (q[4] - kinetic)
        return speeds + [1.4 * pressure * inverse, pressure]

    def store_primitives(q, z):
        values = primitives(q)
        for f in range(5):
            PR[f, z] = values[f]
        return values

    def send_state(r, c, values):
        for f in range(4):
            for k in range(CH // 2):
                XS[0, r, c, f, k] = pack_high(values[k][f], values[k + 2][f])
                XS[1, r, c, f, k] = pack_low(values[k][f], values[k + 2][f])
        YS[r, c, 0] = pack_y([values[k][f] for f in range(4) for k in range(CH)])
        for copy in exchange(r, c):
            copy.start()

    def start_chunk(c, carry):
        values = []
        for k in range(CH):
            z = ghost + c * CH + k
            values.append(store_primitives([QE[f, z] for f in range(5)], z))
        send_state(0, c, values)
        return carry

    def ghost_start():
        near = []
        for z in list(range(ghost)) + list(range(ghost + planes, 2 * ghost + planes)):
            values = store_primitives([QE[f, z] for f in range(5)], z)
            if ghost - 4 <= z < ghost + planes + 4:
                near.append(values)
        for f, field in enumerate((0, 2)):
            for k in range(4):
                XSG[0, f, k] = pack_high(near[k][field], near[k + 4][field])
                XSG[1, f, k] = pack_low(near[k][field], near[k + 4][field])
        YSG[...] = pack_y([near[k][field] for field in (1, 2) for k in range(8)])
        for copy in ghost_exchange():
            copy.start()

    def vertical(z, grads, q, u, p):
        m1, m2, m3, energy = q
        txz, tyz, tzz, heat = grads
        FZ[0, z - 4] = m3
        FZ[1, z - 4] = m1 * u[2] - txz
        FZ[2, z - 4] = m2 * u[2] - tyz
        FZ[3, z - 4] = m3 * u[2] + p - tzz
        FZ[4, z - 4] = (energy + p) * u[2] - (u[0] * txz + u[1] * tyz + u[2] * tzz + heat)

    def flux_chunk(r, c, carry):
        for copy in exchange(r, c):
            copy.wait_recv()
        halos = [[None] * CH for _ in range(4)]
        for f in range(4):
            for k in range(CH // 2):
                halos[f][k], halos[f][k + 2] = unpack_x(XR[0, r, c, f, k], XR[1, r, c, f, k])
        merged = merge_y(YR, r, c, 0)
        packs_x = []
        packs_y = []
        for k in range(CH):
            z = ghost + c * CH + k
            value = [PR[f, z] for f in range(4)]
            gx = [d_x(value[f], halos[f][k]) for f in range(4)]
            gy = [d_y(value[f], unpack_y(merged, CH * f + k)) for f in range(4)]
            gz = [d_z(PR, f, z) for f in range(4)]
            u = value[:3]
            p = PR[4, z]
            m1, m2, m3, energy = [QE[f, z] for f in range(1, 5)]
            dilation = (2.0 / 3.0 * viscosity) * (gx[0] + gy[1] + gz[2])
            txx = (2.0 * viscosity) * gx[0] - dilation
            tyy = (2.0 * viscosity) * gy[1] - dilation
            tzz = (2.0 * viscosity) * gz[2] - dilation
            txy = viscosity * (gx[1] + gy[0])
            txz = viscosity * (gx[2] + gz[0])
            tyz = viscosity * (gy[2] + gz[1])
            total = energy + p
            flux_x = [
                m1,
                m1 * u[0] + p - txx,
                m2 * u[0] - txy,
                m3 * u[0] - txz,
                total * u[0] - (u[0] * txx + u[1] * txy + u[2] * txz + conductivity * gx[3]),
            ]
            flux_y = [
                m2,
                m1 * u[1] - txy,
                m2 * u[1] + p - tyy,
                m3 * u[1] - tyz,
                total * u[1] - (u[0] * txy + u[1] * tyy + u[2] * tyz + conductivity * gy[3]),
            ]
            for f in range(5):
                FX[f, c * CH + k] = flux_x[f]
                FY[f, c * CH + k] = flux_y[f]
            packs_x.append(flux_x)
            packs_y.append(flux_y)
            vertical(z, (txz, tyz, tzz, conductivity * gz[3]), (m1, m2, m3, energy), u, p)
        r = r + 1
        for f in range(5):
            for k in range(CH // 2):
                XS[0, r, c, f, k] = pack_high(packs_x[k][f], packs_x[k + 2][f])
                XS[1, r, c, f, k] = pack_low(packs_x[k][f], packs_x[k + 2][f])
        YS[r, c, 0] = pack_y([packs_y[k][f] for f in range(4) for k in range(CH)])
        YS[r, c, 1] = pack_y([packs_y[k][4] for k in range(CH)])
        for copy in exchange(r, c):
            copy.start()
        return carry

    def ghost_gradients():
        for copy in ghost_exchange():
            copy.wait_recv()
        halos = [[None] * 8 for _ in range(2)]
        for f in range(2):
            for k in range(4):
                halos[f][k], halos[f][k + 4] = unpack_x(XRG[0, f, k], XRG[1, f, k])
        merged = merge_y(YRG)
        for k in range(8):
            z = ghost - 4 + k if k < 4 else ghost + planes + k - 4
            u = [PR[f, z] for f in range(3)]
            GH[0, k] = d_x(u[0], halos[0][k]) + d_y(u[1], unpack_y(merged, k))
            GH[1, k] = d_x(u[2], halos[1][k])
            GH[2, k] = d_y(u[2], unpack_y(merged, 8 + k))

    def ghost_flux(k, carry):
        z = ghost - 4 + k + (planes + 4 - 4) * (k // 4)
        gz = [d_z(PR, f, z) for f in range(4)]
        dilation = (2.0 / 3.0 * viscosity) * (GH[0, k] + gz[2])
        tzz = (2.0 * viscosity) * gz[2] - dilation
        txz = viscosity * (GH[1, k] + gz[0])
        tyz = viscosity * (GH[2, k] + gz[1])
        vertical(
            z,
            (txz, tyz, tzz, conductivity * gz[3]),
            [QE[f, z] for f in range(1, 5)],
            [PR[f, z] for f in range(3)],
            PR[4, z],
        )
        return carry

    def outputs(c):
        return [
            pltpu.make_async_copy(
                QE.at[:, pl.ds(ghost + c * CH, CH)], adv_hbm.at[:, pl.ds(c * CH, CH)], out_sem.at[0, c]
            ),
            pltpu.make_async_copy(REG.at[:, pl.ds(c * CH, CH)], car_hbm.at[:, pl.ds(c * CH, CH)], out_sem.at[1, c]),
        ]

    def update_chunk(section, c, carry):
        r = 2 * section + 1
        for copy in exchange(r, c):
            copy.wait_recv()
        halos = [[None] * CH for _ in range(5)]
        for f in range(5):
            for k in range(CH // 2):
                halos[f][k], halos[f][k + 2] = unpack_x(XR[0, r, c, f, k], XR[1, r, c, f, k])
        merged = [merge_y(YR, r, c, 0), merge_y(YR, r, c, 1)]
        values = []
        for k in range(CH):
            w = c * CH + k
            z = ghost + w
            q = []
            for f in range(5):
                slope = d_x(FX[f, w], halos[f][k])
                slope += d_y(FY[f, w], unpack_y(merged[f // 4], CH * (f % 4) + k))
                slope += d_z(FZ, f, w + 4)
                register = section_a[section] * REG[f, w] - time_step * slope
                REG[f, w] = register
                state = QE[f, z] + section_b[section] * register
                QE[f, z] = state
                q.append(state)
            if section == 0:
                values.append(store_primitives(q, z))
        if section == 0:
            send_state(2, c, values)
        else:
            for copy in outputs(c):
                copy.start()
        return carry

    loads[0].wait()
    pl.semaphore_wait(barrier, 2 + len(y_sides))
    lax.fori_loop(0, chunks, start_chunk, 0)
    loads[1].wait()
    loads[2].wait()
    ghost_start()
    for section in range(2):
        lax.fori_loop(0, chunks, functools.partial(flux_chunk, 2 * section), 0)
        if section == 0:
            ghost_gradients()
            loads[3].wait()
        lax.fori_loop(0, 8, ghost_flux, 0)
        lax.fori_loop(0, chunks, functools.partial(update_chunk, section), 0)

    for copy in ghost_exchange():
        copy.wait_send()

    def finish(c, carry):
        for r in range(4):
            for copy in exchange(r, c):
                copy.wait_send()
        for copy in outputs(c):
            copy.wait()
        return carry

    lax.fori_loop(0, chunks, finish, 0)


def solution(mesh):
    nx, ny = mesh.shape["gx"], mesh.shape["gy"]

    def body(conserved, register, ghost_planes):
        _, planes, rows, columns = conserved.shape
        assert (rows, columns) == (8, 128) and planes % CH == 0
        chunks = planes // CH
        extended = planes + ghost_planes.shape[1]
        tile = (rows, columns)

        def vmem(*shape):
            return pltpu.VMEM(shape + tile, jnp.float32)

        dma = pltpu.SemaphoreType.DMA
        return pl.pallas_call(
            functools.partial(kernel, nx, ny, chunks),
            out_shape=[jax.ShapeDtypeStruct(conserved.shape, jnp.float32)] * 2,
            in_specs=[pl.BlockSpec(memory_space=pl.ANY)] * 3,
            out_specs=[pl.BlockSpec(memory_space=pl.ANY)] * 2,
            scratch_shapes=[
                vmem(5, extended),
                vmem(5, extended),
                vmem(5, planes),
                vmem(5, planes),
                vmem(5, planes),
                vmem(5, planes + 8),
                vmem(3, 8),
                vmem(2, 4, chunks, 5, CH // 2),
                vmem(2, 4, chunks, 5, CH // 2),
                vmem(4, chunks, 2),
                vmem(2, 4, chunks, 2),
                vmem(2, 2, 4),
                vmem(2, 2, 4),
                vmem(),
                vmem(2),
                dma((4,)),
                dma((2, chunks)),
                dma((2, 4, chunks)),
                dma((2, 4, chunks)),
                dma((2, 4, chunks)),
                dma((2, 4, chunks)),
                dma((4,)),
                dma((4,)),
            ],
            compiler_params=pltpu.CompilerParams(
                collective_id=0, has_side_effects=True, vmem_limit_bytes=40 * 1024 * 1024
            ),
        )(conserved, register, ghost_planes)

    spec = P(None, None, "gx", "gy")
    return jax.shard_map(
        body, mesh=mesh, in_specs=(spec, spec, spec), out_specs=(spec, spec), check_vma=False
    )
```

time: 184 us -> 31.8 us (0.17)
  local copies, waits for them, and re-layouts: 64.3 us -> 4.36 us
  other arithmetic: 53.4 us -> 0 us
  waiting for transfers between devices: 45.7 us -> 0 us
  Pallas kernels: 0 us -> 26.6 us
  starting transfers between devices: 16.7 us -> 0 us
    ppermute x16 -> x0, waiting for transfers between devices: 45.7 us -> none  [the longest x8 26.2 us: padded_2(): lax.ppermute(lax.slice_in_dim(block, block.shape[dim] - width, None, axis...]
    slice x26 -> x0, local copies, waits for them, and re-layouts: 35.6 us -> none  [the longest x14 16.6 us: padded_2(): lax.slice_in_dim(block, block.shape[dim] - width, None, axis=dim)]
    sub x18 -> x0, other arithmetic: 33.4 us -> none  [net_flux(): return [inviscid[0]] + [inviscid[k + 1] - viscous[k] for k in range(4)]]
    pallas_call x0 -> x1, Pallas kernels: none -> 26.6 us  [body(): pl.pallas_call(functools.partial(kernel, nx, ny, chunks), out_shape=[jax....]
    ppermute x16 -> x0, local copies, waits for them, and re-layouts: 17.1 us -> none  [the longest x8 10.7 us: padded_2(): lax.ppermute(lax.slice_in_dim(block, block.shape[dim] - width, None, axis...]
    ppermute x16 -> x0, starting transfers between devices: 16.7 us -> none  [the longest x8 12 us: padded_2(): lax.ppermute(lax.slice_in_dim(block, 0, width, axis=dim), axis, backward)]
    concatenate x8 -> x0, other arithmetic: 8.39 us -> none  [the longest x6 7.32 us: padded_2(): block = jnp.concatenate([low, block, high], axis=dim)]
    unnamed x16 -> x0, other arithmetic: 7.64 us -> none
  transfers between devices with their start and end apart: 16 -> 0, of which waited for: 16 -> 0; matrix products, arithmetic and copies ran while one was open for 17% -> 0% of each run, Pallas kernels for 0% -> 0%
where the time goes in v1:
time: 31.8 us; the launch traced here: 31.6 us
  Pallas kernels  26.6 us (84%)
  local copies, waits for them, and re-layouts  4.36 us (14%)
  between operations  0.65 us (2%)
    pallas_call x1, Pallas kernels, body(): pl.pallas_call(functools.partial(kernel, nx, ny, chunks), out_shape=[jax....  26.6 us
    unnamed x8, local copies, waits for them, and re-layouts  4.36 us

profile of v1, /device:TPU:0, one launch (start us, length us, event | category | flops | bytes accessed | tf_op | source)
XLA Modules:
  0.0 31.6 jit_solution(4609167966437235858)
XLA Ops:
  0.6 0.0 copy-start
  0.6 1.0 %copy-done = f32[5,16,8,128]{3,2,1,0:T(8,128)S(1)} copy-done((f32[5,16,8,128]{3,2,1,0:T(8,128)S(1)}, f32[5,16,8,128]{3,2,1,0:T(8,128)}, u32[]{:S(2)}) %copy-start) | copy-done | bytes 327704
  1.6 0.0 copy-start.1
  1.6 1.0 %copy-done.1 = f32[5,16,8,128]{3,2,1,0:T(8,128)S(1)} copy-done((f32[5,16,8,128]{3,2,1,0:T(8,128)S(1)}, f32[5,16,8,128]{3,2,1,0:T(8,128)}, u32[]{:S(2)}) %copy-start.1) | copy-done | bytes 327704
  2.6 0.0 copy-start.2
  2.6 1.0 %copy-done.2 = f32[5,16,8,128]{3,2,1,0:T(8,128)S(1)} copy-done((f32[5,16,8,128]{3,2,1,0:T(8,128)S(1)}, f32[5,16,8,128]{3,2,1,0:T(8,128)}, u32[]{:S(2)}) %copy-start.2) | copy-done | bytes 327704
  3.5 26.6 %shard_map.50 = (f32[5,16,8,128]{3,2,1,0:T(8,128)S(1)}, f32[5,16,8,128]{3,2,1,0:T(8,128)S(1)}) custom-call(f32[5,16,8,128]{3,2,1,0:T(8,128)S(1)} %copy-done, f32[5,16,8,128]{3,2,1,0:T(8,128)S(1)} %copy-done.1, f32[5,16,8,128]{3,2,1,0:T(8,128)S(1)} %copy-done.2), custom_call_target="tpu_custom_call" | custom-call | tf_op jit(solution)/shard_map/pallas_call | solution.py:410
  30.2 0.7 %copy.7 = f32[5,16,8,128]{3,2,1,0:T(8,128)} copy(f32[5,16,8,128]{3,2,1,0:T(8,128)S(1)} %get-tuple-element.4) | data formatting | bytes 655360
  30.9 0.7 %copy.8 = f32[5,16,8,128]{3,2,1,0:T(8,128)} copy(f32[5,16,8,128]{3,2,1,0:T(8,128)S(1)} %get-tuple-element.5) | data formatting | bytes 655360
Async XLA Ops:
  0.6 1.0 %copy-start = (f32[5,16,8,128]{3,2,1,0:T(8,128)S(1)}, f32[5,16,8,128]{3,2,1,0:T(8,128)}, u32[]{:S(2)}) copy-start(f32[5,16,8,128]{3,2,1,0:T(8,128)} %cons_hbm.1) | copy-start | bytes 983044
  1.6 1.0 %copy-start.1 = (f32[5,16,8,128]{3,2,1,0:T(8,128)S(1)}, f32[5,16,8,128]{3,2,1,0:T(8,128)}, u32[]{:S(2)}) copy-start(f32[5,16,8,128]{3,2,1,0:T(8,128)} %reg_hbm.1) | copy-start | bytes 983044
  2.6 1.0 %copy-start.2 = (f32[5,16,8,128]{3,2,1,0:T(8,128)S(1)}, f32[5,16,8,128]{3,2,1,0:T(8,128)}, u32[]{:S(2)}) copy-start(f32[5,16,8,128]{3,2,1,0:T(8,128)} %ghost_hbm.1) | copy-start | bytes 983044

commit v2 on v1

--- a/solution.py
+++ b/solution.py
@@ -16,6 +16,9 @@
 section_b = (0.37921031, 0.82295503)
 stencil = (0.8, -0.2, 4.0 / 105.0, -1.0 / 280.0)
 CH = 4
+HALF = CH // 2
+Y_STATE = (4 * CH + 15) // 16
+Y_FLUX = (5 * CH + 15) // 16
 
 
 def kernel(
@@ -25,8 +28,9 @@
     cons_hbm,
     reg_hbm,
     ghost_hbm,
-    adv_hbm,
-    car_hbm,
+    state_out,
+    register_out,
+    slope_out,
     QE,
     PR,
     REG,
@@ -34,6 +38,10 @@
     FY,
     FZ,
     GH,
+    DX,
+    DY,
+    DZ,
+    SL,
     XS,
     XR,
     YS,
@@ -43,7 +51,6 @@
     YSG,
     YRG,
     in_sem,
-    out_sem,
     xs_sem,
     xr_sem,
     ys_sem,
@@ -125,7 +132,7 @@
         )
 
     def exchange(r, c):
-        fields, count = ((4, 1), (5, 2))[r % 2]
+        fields, count = ((4, Y_STATE), (5, Y_FLUX))[r % 2]
         return [x_send(way, r, c, fields) for way in (0, 1)] + [y_send(way, r, c, count) for way in y_sides]
 
     def ghost_exchange():
@@ -141,6 +148,52 @@
         first = jnp.where(low, from_right, from_left)
         second = pltpu.roll(jnp.where(low, from_left, from_right), 4, 0)
         return first, second
+
+    row = lax.bitwise_and(sub, 3)
+    column = lax.bitwise_and(lane, 7)
+    edge = jnp.logical_or(lane < 4, lane >= 124)
+    low_weights = [jnp.where(row + d <= 3, -stencil[3 - d], 0.0) for d in range(4)]
+    high_weights = [jnp.where(row >= d, stencil[3 - d], 0.0) for d in range(4)]
+
+    def inner_x(field):
+        a, b, c, _ = stencil
+        after = pltpu.roll(field, 7, 0)
+        before = pltpu.roll(field, 1, 0)
+        middle = b * field
+        return pltpu.roll(a * before + middle + c * after, 6, 0) - pltpu.roll(a * after + middle + c * before, 2, 0)
+
+    def inner_y(field):
+        a, b, c, d = stencil
+        after = pltpu.roll(field, 127, 1)
+        before = pltpu.roll(field, 1, 1)
+        middle = c * field
+        far = pltpu.roll(b * before + middle + d * after, 125, 1) - pltpu.roll(b * after + middle + d * before, 3, 1)
+        return a * (after - before) + far
+
+    def edge_x(r, c, f, k):
+        gap_low = XR[0, r, c, f, k] - XS[0, r, c, f, k]
+        gap_high = XR[1, r, c, f, k] - XS[1, r, c, f, k]
+        at_low = low_weights[0] * gap_low
+        at_high = high_weights[0] * gap_high
+        for d in range(1, 4):
+            at_low += low_weights[d] * pltpu.roll(gap_low, 8 - d, 0)
+            at_high += high_weights[d] * pltpu.roll(gap_high, d, 0)
+        return pltpu.roll(jnp.where(low, at_high, at_low), 4, 0), jnp.where(low, at_low, at_high)
+
+    def edge_y(merged, own):
+        gap = merged - own
+        total = None
+        for o, weight in enumerate(stencil, start=1):
+            at_high = jnp.logical_and(column < 4, column + o >= 4)
+            at_low = jnp.logical_and(column >= 4, column - o < 4)
+            term = jnp.where(at_high, weight, 0.0) * pltpu.roll(gap, 128 - o, 1)
+            term += jnp.where(at_low, -weight, 0.0) * pltpu.roll(gap, o, 1)
+            total = term if total is None else total + term
+        return total
+
+    def place_y(packed, j):
+        packed, j = packed[j // 16], j % 16
+        return jnp.where(edge, pltpu.roll(packed, (128 - (8 * j + 4)) % 128, 1), 0.0)
 
     def pack_y(items):
         packed = None
@@ -149,6 +202,10 @@
             packed = turned if packed is None else jnp.where(lane_group == j, turned, packed)
         return packed
 
+    def send_y(r, c, items):
+        for i in range(0, len(items), 16):
+            YS[r, c, i // 16] = pack_y(items[i : i + 16])
+
     def merge_y(ref, *index):
         if ny == 2:
             return ref[(0,) + index]
@@ -159,13 +216,12 @@
 
     def d_x(field, halo):
         total = None
-        for s, weight in enumerate(stencil[:3], start=1):
+        for s, weight in enumerate(stencil, start=1):
             plus = pltpu.roll(jnp.where(sub < s, halo, field), 8 - s, 0)
             minus = pltpu.roll(jnp.where(sub >= 8 - s, halo, field), s, 0)
             term = weight * (plus - minus)
             total = term if total is None else total + term
-        gap = halo - field
-        return total + stencil[3] * pltpu.roll(jnp.where(low, gap, -gap), 4, 0)
+        return total
 
     def d_y(field, halo):
         total = None
@@ -198,10 +254,10 @@
 
     def send_state(r, c, values):
         for f in range(4):
-            for k in range(CH // 2):
-                XS[0, r, c, f, k] = pack_high(values[k][f], values[k + 2][f])
-                XS[1, r, c, f, k] = pack_low(values[k][f], values[k + 2][f])
-        YS[r, c, 0] = pack_y([values[k][f] for f in range(4) for k in range(CH)])
+            for k in range(HALF):
+                XS[0, r, c, f, k] = pack_high(values[k][f], values[k + HALF][f])
+                XS[1, r, c, f, k] = pack_low(values[k][f], values[k + HALF][f])
+        send_y(r, c, [values[k][f] for f in range(4) for k in range(CH)])
         for copy in exchange(r, c):
             copy.start()
 
@@ -236,22 +292,33 @@
         FZ[3, z - 4] = m3 * u[2] + p - tzz
         FZ[4, z - 4] = (energy + p) * u[2] - (u[0] * txz + u[1] * tyz + u[2] * tzz + heat)
 
+    def gradient_chunk(c, carry):
+        for k in range(CH):
+            w = c * CH + k
+            for f in range(4):
+                field = PR[f, ghost + w]
+                DX[f, w] = inner_x(field)
+                DY[f, w] = inner_y(field)
+                DZ[f, w] = d_z(PR, f, ghost + w)
+        return carry
+
     def flux_chunk(r, c, carry):
         for copy in exchange(r, c):
             copy.wait_recv()
-        halos = [[None] * CH for _ in range(4)]
+        edges = [[None] * CH for _ in range(4)]
         for f in range(4):
-            for k in range(CH // 2):
-                halos[f][k], halos[f][k + 2] = unpack_x(XR[0, r, c, f, k], XR[1, r, c, f, k])
-        merged = merge_y(YR, r, c, 0)
+            for k in range(HALF):
+                edges[f][k], edges[f][k + HALF] = edge_x(r, c, f, k)
+        packed = [edge_y(merge_y(YR, r, c, i), YS[r, c, i]) for i in range(Y_STATE)]
         packs_x = []
         packs_y = []
         for k in range(CH):
             z = ghost + c * CH + k
             value = [PR[f, z] for f in range(4)]
-            gx = [d_x(value[f], halos[f][k]) for f in range(4)]
-            gy = [d_y(value[f], unpack_y(merged, CH * f + k)) for f in range(4)]
-            gz = [d_z(PR, f, z) for f in range(4)]
+            w = c * CH + k
+            gx = [DX[f, w] + edges[f][k] for f in range(4)]
+            gy = [DY[f, w] + place_y(packed, CH * f + k) for f in range(4)]
+            gz = [DZ[f, w] for f in range(4)]
             u = value[:3]
             p = PR[4, z]
             m1, m2, m3, energy = [QE[f, z] for f in range(1, 5)]
@@ -278,18 +345,17 @@
                 total * u[1] - (u[0] * txy + u[1] * tyy + u[2] * tyz + conductivity * gy[3]),
             ]
             for f in range(5):
-                FX[f, c * CH + k] = flux_x[f]
-                FY[f, c * CH + k] = flux_y[f]
+                FX[f, w] = flux_x[f]
+                FY[f, w] = flux_y[f]
             packs_x.append(flux_x)
             packs_y.append(flux_y)
             vertical(z, (txz, tyz, tzz, conductivity * gz[3]), (m1, m2, m3, energy), u, p)
         r = r + 1
         for f in range(5):
-            for k in range(CH // 2):
-                XS[0, r, c, f, k] = pack_high(packs_x[k][f], packs_x[k + 2][f])
-                XS[1, r, c, f, k] = pack_low(packs_x[k][f], packs_x[k + 2][f])
-        YS[r, c, 0] = pack_y([packs_y[k][f] for f in range(4) for k in range(CH)])
-        YS[r, c, 1] = pack_y([packs_y[k][4] for k in range(CH)])
+            for k in range(HALF):
+                XS[0, r, c, f, k] = pack_high(packs_x[k][f], packs_x[k + HALF][f])
+                XS[1, r, c, f, k] = pack_low(packs_x[k][f], packs_x[k + HALF][f])
+        send_y(r, c, [packs_y[k][f] for f in range(5) for k in range(CH)])
         for copy in exchange(r, c):
             copy.start()
         return carry
@@ -325,44 +391,42 @@
         )
         return carry
 
-    def outputs(c):
-        return [
-            pltpu.make_async_copy(
-                QE.at[:, pl.ds(ghost + c * CH, CH)], adv_hbm.at[:, pl.ds(c * CH, CH)], out_sem.at[0, c]
-            ),
-            pltpu.make_async_copy(REG.at[:, pl.ds(c * CH, CH)], car_hbm.at[:, pl.ds(c * CH, CH)], out_sem.at[1, c]),
-        ]
+    def slope_chunk(c, carry):
+        for k in range(CH):
+            w = c * CH + k
+            for f in range(5):
+                SL[f, w] = inner_x(FX[f, w]) + inner_y(FY[f, w]) + d_z(FZ, f, w + 4)
+        return carry
 
     def update_chunk(section, c, carry):
         r = 2 * section + 1
         for copy in exchange(r, c):
             copy.wait_recv()
-        halos = [[None] * CH for _ in range(5)]
+        edges = [[None] * CH for _ in range(5)]
         for f in range(5):
-            for k in range(CH // 2):
-                halos[f][k], halos[f][k + 2] = unpack_x(XR[0, r, c, f, k], XR[1, r, c, f, k])
-        merged = [merge_y(YR, r, c, 0), merge_y(YR, r, c, 1)]
+            for k in range(HALF):
+                edges[f][k], edges[f][k + HALF] = edge_x(r, c, f, k)
+        packed = [edge_y(merge_y(YR, r, c, i), YS[r, c, i]) for i in range(Y_FLUX)]
         values = []
         for k in range(CH):
             w = c * CH + k
             z = ghost + w
             q = []
             for f in range(5):
-                slope = d_x(FX[f, w], halos[f][k])
-                slope += d_y(FY[f, w], unpack_y(merged[f // 4], CH * (f % 4) + k))
-                slope += d_z(FZ, f, w + 4)
-                register = section_a[section] * REG[f, w] - time_step * slope
-                REG[f, w] = register
-                state = QE[f, z] + section_b[section] * register
+                slope = SL[f, w] + edges[f][k] + place_y(packed, CH * f + k)
+                if section == 1:
+                    slope_out[f, w] = slope
+                    continue
+                register = section_a[0] * REG[f, w] - time_step * slope
+                register_out[f, w] = register
+                state = QE[f, z] + section_b[0] * register
                 QE[f, z] = state
+                state_out[f, w] = state
                 q.append(state)
             if section == 0:
                 values.append(store_primitives(q, z))
         if section == 0:
             send_state(2, c, values)
-        else:
-            for copy in outputs(c):
-                copy.start()
         return carry
 
     loads[0].wait()
@@ -372,11 +436,13 @@
     loads[2].wait()
     ghost_start()
     for section in range(2):
+        lax.fori_loop(0, chunks, gradient_chunk, 0)
         lax.fori_loop(0, chunks, functools.partial(flux_chunk, 2 * section), 0)
         if section == 0:
             ghost_gradients()
             loads[3].wait()
         lax.fori_loop(0, 8, ghost_flux, 0)
+        lax.fori_loop(0, chunks, slope_chunk, 0)
         lax.fori_loop(0, chunks, functools.partial(update_chunk, section), 0)
 
     for copy in ghost_exchange():
@@ -386,8 +452,6 @@
         for r in range(4):
             for copy in exchange(r, c):
                 copy.wait_send()
-        for copy in outputs(c):
-            copy.wait()
         return carry
 
     lax.fori_loop(0, chunks, finish, 0)
@@ -407,11 +471,11 @@
             return pltpu.VMEM(shape + tile, jnp.float32)
 
         dma = pltpu.SemaphoreType.DMA
-        return pl.pallas_call(
+        state, old, slope = pl.pallas_call(
             functools.partial(kernel, nx, ny, chunks),
-            out_shape=[jax.ShapeDtypeStruct(conserved.shape, jnp.float32)] * 2,
-            in_specs=[pl.BlockSpec(memory_space=pl.ANY)] * 3,
-            out_specs=[pl.BlockSpec(memory_space=pl.ANY)] * 2,
+            out_shape=[pltpu.VMEM(conserved.shape, jnp.float32)] * 3,
+            in_specs=[pl.BlockSpec(memory_space=pltpu.HBM)] * 3,
+            out_specs=[pl.BlockSpec(memory_space=pltpu.VMEM)] * 3,
             scratch_shapes=[
                 vmem(5, extended),
                 vmem(5, extended),
@@ -420,16 +484,19 @@
                 vmem(5, planes),
                 vmem(5, planes + 8),
                 vmem(3, 8),
-                vmem(2, 4, chunks, 5, CH // 2),
-                vmem(2, 4, chunks, 5, CH // 2),
-                vmem(4, chunks, 2),
-                vmem(2, 4, chunks, 2),
+                vmem(4, planes),
+                vmem(4, planes),
+                vmem(4, planes),
+                vmem(5, planes),
+                vmem(2, 4, chunks, 5, HALF),
+                vmem(2, 4, chunks, 5, HALF),
+                vmem(4, chunks, Y_FLUX),
+                vmem(2, 4, chunks, Y_FLUX),
                 vmem(2, 2, 4),
                 vmem(2, 2, 4),
                 vmem(),
                 vmem(2),
                 dma((4,)),
-                dma((2, chunks)),
                 dma((2, 4, chunks)),
                 dma((2, 4, chunks)),
                 dma((2, 4, chunks)),
@@ -438,9 +505,11 @@
                 dma((4,)),
             ],
             compiler_params=pltpu.CompilerParams(
-                collective_id=0, has_side_effects=True, vmem_limit_bytes=40 * 1024 * 1024
+                collective_id=0, has_side_effects=True, vmem_limit_bytes=60 * 1024 * 1024
             ),
         )(conserved, register, ghost_planes)
+        carried = section_a[1] * old - time_step * slope
+        return state + section_b[1] * carried, carried
 
     spec = P(None, None, "gx", "gy")
     return jax.shard_map(

time: 31.8 us -> 26.4 us (0.83)
  local copies, waits for them, and re-layouts: 4.36 us -> 0 us
  Pallas kernels: 26.6 us -> 24.7 us
  other arithmetic: 0 us -> 0.91 us
    unnamed x8 -> x0, local copies, waits for them, and re-layouts: 4.36 us -> none
    pallas_call x1, Pallas kernels: 26.6 us -> 24.7 us  [body(): pl.pallas_call(functools.partial(kernel, nx, ny, chunks), out_shape=[pltp...]
    add x0 -> x1, other arithmetic: none -> 0.91 us  [body(): return (state + section_b[1] * carried, carried)]
where the time goes in v2:
time: 26.4 us; the launch traced here: 26.3 us
  Pallas kernels  24.7 us (94%)
  other arithmetic  0.91 us (3%)
  between operations  0.64 us (2%)
    pallas_call x1, Pallas kernels, body(): pl.pallas_call(functools.partial(kernel, nx, ny, chunks), out_shape=[pltp...  24.7 us
    add x1, other arithmetic, body(): return (state + section_b[1] * carried, carried)  0.91 us

profile of v2, /device:TPU:0, one launch (start us, length us, event | category | flops | bytes accessed | tf_op | source)
XLA Modules:
  0.0 26.3 jit_solution(4051837668722415016)
XLA Ops:
  0.6 24.7 %shard_map.50 = (f32[5,16,8,128]{3,2,1,0:T(8,128)S(1)}, f32[5,16,8,128]{3,2,1,0:T(8,128)S(1)}, f32[5,16,8,128]{3,2,1,0:T(8,128)S(1)}) custom-call(f32[5,16,8,128]{3,2,1,0:T(8,128)} %cons_hbm.1, f32[5,16,8,128]{3,2,1,0:T(8,128)} %reg_hbm.1, f32[5,16,8,128]{3,2,1,0:T(8,128)} %ghost_hbm.1), custom_call_target="tpu_custom_call" | custom-call | tf_op jit(solution)/shard_map/pallas_call | solution.py:474
  25.4 0.9 %multiply_add_fusion = (f32[5,16,8,128]{3,2,1,0:T(8,128)}, f32[5,16,8,128]{3,2,1,0:T(8,128)}) fusion(f32[5,16,8,128]{3,2,1,0:T(8,128)S(1)} %get-tuple-element.5, f32[5,16,8,128]{3,2,1,0:T(8,128)S(1)} %get-tuple-element.7, f32[5,16,8,128]{3,2,1,0:T(8,128)S(1)} %get-tuple-element.6), kind=kLoop, calls=%fused_computation | loop fusion | flops 409600 | bytes 1638400 | tf_op jit(solution)/shard_map/add | solution.py:512

commit v3 on v2

--- a/solution.py
+++ b/solution.py
@@ -257,8 +257,11 @@
             for k in range(HALF):
                 XS[0, r, c, f, k] = pack_high(values[k][f], values[k + HALF][f])
                 XS[1, r, c, f, k] = pack_low(values[k][f], values[k + HALF][f])
+        copies = exchange(r, c)
+        for copy in copies[:2]:
+            copy.start()
         send_y(r, c, [values[k][f] for f in range(4) for k in range(CH)])
-        for copy in exchange(r, c):
+        for copy in copies[2:]:
             copy.start()
 
     def start_chunk(c, carry):
@@ -312,6 +315,7 @@
         packed = [edge_y(merge_y(YR, r, c, i), YS[r, c, i]) for i in range(Y_STATE)]
         packs_x = []
         packs_y = []
+        downs = []
         for k in range(CH):
             z = ghost + c * CH + k
             value = [PR[f, z] for f in range(4)]
@@ -344,20 +348,25 @@
                 m3 * u[1] - tyz,
                 total * u[1] - (u[0] * txy + u[1] * tyy + u[2] * tyz + conductivity * gy[3]),
             ]
-            for f in range(5):
-                FX[f, w] = flux_x[f]
-                FY[f, w] = flux_y[f]
             packs_x.append(flux_x)
             packs_y.append(flux_y)
-            vertical(z, (txz, tyz, tzz, conductivity * gz[3]), (m1, m2, m3, energy), u, p)
+            downs.append((z, (txz, tyz, tzz, conductivity * gz[3]), (m1, m2, m3, energy), u, p))
         r = r + 1
+        copies = exchange(r, c)
         for f in range(5):
             for k in range(HALF):
                 XS[0, r, c, f, k] = pack_high(packs_x[k][f], packs_x[k + HALF][f])
                 XS[1, r, c, f, k] = pack_low(packs_x[k][f], packs_x[k + HALF][f])
+        for copy in copies[:2]:
+            copy.start()
         send_y(r, c, [packs_y[k][f] for f in range(5) for k in range(CH)])
-        for copy in exchange(r, c):
+        for copy in copies[2:]:
             copy.start()
+        for k in range(CH):
+            for f in range(5):
+                FX[f, c * CH + k] = packs_x[k][f]
+                FY[f, c * CH + k] = packs_y[k][f]
+            vertical(*downs[k])
         return carry
 
     def ghost_gradients():

time: 26.4 us -> 26.1 us (0.989)
  Pallas kernels: 24.7 us -> 24.4 us
    pallas_call x1, Pallas kernels: 24.7 us -> 24.4 us  [body(): pl.pallas_call(functools.partial(kernel, nx, ny, chunks), out_shape=[pltp...]
where the time goes in v3:
time: 26.1 us; the launch traced here: 26 us
  Pallas kernels  24.4 us (93%)
  other arithmetic  0.91 us (3%)
  between operations  0.64 us (2%)
    pallas_call x1, Pallas kernels, body(): pl.pallas_call(functools.partial(kernel, nx, ny, chunks), out_shape=[pltp...  24.4 us
    add x1, other arithmetic, body(): return (state + section_b[1] * carried, carried)  0.91 us

profile of v3, /device:TPU:0, one launch (start us, length us, event | category | flops | bytes accessed | tf_op | source)
XLA Modules:
  0.0 26.0 jit_solution(9590758512570379184)
XLA Ops:
  0.6 24.4 %shard_map.50 = (f32[5,16,8,128]{3,2,1,0:T(8,128)S(1)}, f32[5,16,8,128]{3,2,1,0:T(8,128)S(1)}, f32[5,16,8,128]{3,2,1,0:T(8,128)S(1)}) custom-call(f32[5,16,8,128]{3,2,1,0:T(8,128)} %cons_hbm.1, f32[5,16,8,128]{3,2,1,0:T(8,128)} %reg_hbm.1, f32[5,16,8,128]{3,2,1,0:T(8,128)} %ghost_hbm.1), custom_call_target="tpu_custom_call" | custom-call | tf_op jit(solution)/shard_map/pallas_call | solution.py:483
  25.1 0.9 %multiply_add_fusion = (f32[5,16,8,128]{3,2,1,0:T(8,128)}, f32[5,16,8,128]{3,2,1,0:T(8,128)}) fusion(f32[5,16,8,128]{3,2,1,0:T(8,128)S(1)} %get-tuple-element.5, f32[5,16,8,128]{3,2,1,0:T(8,128)S(1)} %get-tuple-element.7, f32[5,16,8,128]{3,2,1,0:T(8,128)S(1)} %get-tuple-element.6), kind=kLoop, calls=%fused_computation | loop fusion | flops 409600 | bytes 1638400 | tf_op jit(solution)/shard_map/add | solution.py:521
